TPU v7x, 32 devices: a whole 2x2x4 slice. The times are simulated.
32 devices in a mesh: section: 4 (over z), sector: 4 (over y, core), comp: 2 (over x).
Axes of the slice: x: 2, y: 2, z: 4, core: 2. Of those that a mesh axis runs over, the one named last changes fastest.
Arguments:
- env_in: bfloat16 [2, 8, 4, 512, 128], P('comp', None, 'sector', 'section'), may hold values from -6 to 6
- site_tensor: bfloat16 [3, 4, 512, 4, 512], P(None, 'sector', None, None, 'section'), may hold values from -0.125 to 0.125
- bra_tensor: bfloat16 [3, 4, 128, 4, 128], P(None, 'sector'), may hold values from -0.5 to 0.5
- mixing: float32 [3, 4, 8, 8], replicated, may hold values from -2 to 2
- sector_sizes: int32 [4, 4], replicated, may hold values from 256 to 512, as said below
- targets: int32 [3, 4, 4], replicated, may hold values from 0 to 3, as said below
Outputs:
- env_out: bfloat16 [3, 2, 8, 4, 512, 128], P(None, 'comp', None, 'sector', 'section')
- total_env: bfloat16 [8, 4, 512, 128], P('comp', 'sector', 'section')
Inputs may be any that keep to these rules, and one draw needn't show every extreme that they name: `sector_sizes`: on every bond some sector has exactly 512 states. For each site and source sector a the 4 targets are distinct and differ from a by at most 3; at every site some target lies 3 above its source sector and some 3 below.
All inputs are finite; a program needn't handle non-finite values.
Results may differ from a plain program's by a relative error of at most 0.02.
Values may be sent and summed in bfloat16 or wider, within the bound.
A program may use at most 64 MiB of HBM per device.

v0:
```python
import jax
import jax.numpy as jnp
from jax import lax
from jax.sharding import PartitionSpec as P


def local(env_in, site_tensor, bra_tensor, mixing, sector_sizes, targets):
    section_index = lax.axis_index("section")
    sector_index = lax.axis_index("sector")
    sector_count = lax.axis_size("sector")
    site_count = site_tensor.shape[0]
    full_rows = site_tensor.shape[2]
    local_rows = site_tensor.shape[4]
    row_ids = jnp.arange(full_rows, dtype=jnp.int32)
    own_rows = section_index * local_rows + jnp.arange(local_rows, dtype=jnp.int32)
    keep_first = (own_rows < sector_sizes[0, sector_index]).astype(jnp.bfloat16)
    current = env_in[:, :, 0] * keep_first[None, None, :, None]
    results = []
    for site_index in range(site_count):
        targets_row = targets[site_index, sector_index]
        size_out = sector_sizes[site_index + 1][targets_row]
        keep_in = (row_ids < sector_sizes[site_index, sector_index]).astype(jnp.bfloat16)
        keep_out = (own_rows[None, :] < size_out[:, None]).astype(jnp.bfloat16)
        masked = site_tensor[site_index, 0] * keep_in[:, None, None] * keep_out[None, :, :]
        weights = mixing[site_index]
        mixed_rows = jnp.einsum(
            "sdc,bcik->bdsik",
            weights,
            lax.all_gather(current, "section", axis=2, tiled=True).astype(jnp.float32),
            precision=lax.Precision.HIGHEST,
        ).astype(jnp.bfloat16)
        left_total = jnp.einsum(
            "iso,bdsik->bdsok", masked, mixed_rows, preferred_element_type=jnp.float32
        )
        left_part = left_total.astype(jnp.bfloat16)
        partial_value = jnp.einsum(
            "bdsok,ksl->bdsol",
            left_part,
            bra_tensor[site_index, 0],
            preferred_element_type=jnp.float32,
        ).astype(jnp.bfloat16)
        onehot = (
            targets_row[None, :] == jnp.arange(sector_count, dtype=jnp.int32)[:, None]
        ).astype(jnp.bfloat16)
        outgoing = jnp.einsum(
            "js,bdsol->jbdol", onehot, partial_value, preferred_element_type=jnp.float32
        ).astype(jnp.bfloat16)
        received = lax.all_to_all(outgoing, "sector", split_axis=0, concat_axis=0, tiled=True)
        updated = jnp.sum(received, axis=0, dtype=jnp.float32)
        current = updated.astype(jnp.bfloat16)
        results.append(current)
    stacked = jnp.stack(results)[:, :, :, None]
    batch_term = jnp.sum(current.astype(jnp.float32), axis=0)
    summed = lax.psum_scatter(
        batch_term.astype(jnp.bfloat16), "comp", scatter_dimension=0, tiled=True
    )
    return (stacked, summed[:, None])


def solution(mesh):
    in_specs = (
        P("comp", None, "sector", "section", None),
        P(None, "sector", None, None, "section"),
        P(None, "sector", None, None, None),
        P(),
        P(),
        P(),
    )
    out_specs = (
        P(None, "comp", None, "sector", "section", None),
        P("comp", "sector", "section", None),
    )
    return jax.shard_map(local, mesh=mesh, in_specs=in_specs, out_specs=out_specs, check_vma=False)
```

profile of v0, /device:TPU:0, one launch (start us, length us, event | category | flops | bytes accessed | tf_op | source)
XLA Modules:
  0.0 202.3 jit_solution(12540820073185199314)
XLA Ops:
  7.2 1.5 constant_dynamic-slice_fusion.4
  9.3 1.9 bitcast_multiply_fusion.3
  16.1 1.3 fusion.65
  17.5 1.2 fusion.78
  18.6 2.8 %fusion.45 = (bf16[512,4,128,1]{2,1,0,3:T(4,128)(2,1)S(1)}, bf16[512,4,128,1]{2,1,0,3:T(4,128)(2,1)S(1)}, bf16[512,4,128,1]{2,1,0,3:T(4,128)(2,1)S(1)}) fusion(bf16[3,1,512,4,128]{4,3,2,1,0:T(4,128)(2,1)S(1)} %copy-done, bf16[512]{0:T(512)(128)(2,1)S(1)} %get-tuple-element.32, bf16[4,128]{1,0:T(4,128)(2,1)S(1)} %get-tuple-element.26, ...), kind=kLoop, calls=%fused_computation.40 | loop fusion | flops 1572864 | bytes 3151872 | tf_op jit(solution)/shard_map/mul | solution.py:24
  21.5 20.5 %all-gather.6.cloned.1.call-done = bf16[1,8,512,128]{3,1,0,2:T(8,128)(2,1)} async-done(((bf16[1,8,128,128]{3,1,0,2:T(8,128)(2,1)}), bf16[1,8,512,128]{3,1,0,2:T(8,128)(2,1)}) %all-gather.6.cloned.1.call-update) | async-done | bytes 1048592 | tf_op jit(solution)/shard_map/all_gather | solution.py:29
  42.0 6.6 %convert_bitcast_fusion.2 = bf16[8,4,512,128]{3,0,1,2:T(8,128)(2,1)} fusion(bf16[1,8,512,128]{3,1,0,2:T(8,128)(2,1)} %all-gather.6.cloned.1.call-done, f32[3,4,8,8]{3,2,1,0:T(8,128)} %param.9), kind=kOutput, calls=%fused_computation.11 | convolution fusion | flops 203423744 | bytes 5259264 | tf_op jit(solution)/shard_map/sdc,bcik->bdsik/dot_general | solution.py:26
  48.6 4.4 %fusion.15 = bf16[8,4,128,128]{3,2,0,1:T(8,128)(2,1)S(1)} fusion(bf16[8,4,512,128]{3,0,1,2:T(8,128)(2,1)} %convert_bitcast_fusion.2, bf16[512,4,128,1]{2,1,0,3:T(4,128)(2,1)S(1)} %get-tuple-element.9, bf16[1,1,128,4,128]{4,3,2,1,0:T(4,128)(2,1)S(1)} %get-tuple-element.13), kind=kOutput, calls=%fused_computation.21 | convolution fusion | flops 672137216 | bytes 5898240 | tf_op jit(solution)/shard_map/bdsok,ksl->bdsol/dot_general | solution.py:36
  53.0 0.9 fusion.16
  54.2 17.0 %all_to_all.15 = bf16[4,1,8,128,128]{4,3,2,1,0:T(8,128)(2,1)S(1)} all-to-all(bf16[4,1,8,128,128]{4,3,2,1,0:T(8,128)(2,1)S(1)} %copy.50), channel_id=1, replica_groups=mesh['section'=4,'sector'=4,'comp'=2] {'sector'}, dimensions={0} | all-to-all | bytes 2097152 | tf_op jit(solution)/shard_map/all_to_all | solution.py:48
  71.4 0.9 copy.52
  72.5 26.4 %all-gather.8.cloned.1.call-done = bf16[8,512,128]{2,0,1:T(8,128)(2,1)} async-done(((bf16[8,128,128]{2,0,1:T(8,128)(2,1)}), bf16[8,512,128]{2,0,1:T(8,128)(2,1)}) %all-gather.8.cloned.1.call-update) | async-done | bytes 1048592 | tf_op jit(solution)/shard_map/all_gather | solution.py:29
  99.0 6.2 %convert_bitcast_fusion.1 = bf16[8,4,512,128]{3,0,1,2:T(8,128)(2,1)} fusion(bf16[8,512,128]{2,0,1:T(8,128)(2,1)} %all-gather.8.cloned.1.call-done, f32[3,4,8,8]{3,2,1,0:T(8,128)S(1)} %copy-done.1), kind=kOutput, calls=%fused_computation.10 | convolution fusion | flops 203423744 | bytes 5259264 | tf_op jit(solution)/shard_map/sdc,bcik->bdsik/dot_general | solution.py:26
  105.2 4.4 %fusion.17 = bf16[8,4,128,128]{3,2,0,1:T(8,128)(2,1)S(1)} fusion(bf16[8,4,512,128]{3,0,1,2:T(8,128)(2,1)} %convert_bitcast_fusion.1, bf16[512,4,128,1]{2,1,0,3:T(4,128)(2,1)S(1)} %get-tuple-element.10, bf16[1,1,128,4,128]{4,3,2,1,0:T(4,128)(2,1)S(1)} %get-tuple-element.12), kind=kOutput, calls=%fused_computation.23 | convolution fusion | flops 672137216 | bytes 5898240 | tf_op jit(solution)/shard_map/bdsok,ksl->bdsol/dot_general | solution.py:36
  109.6 0.9 fusion.18
  110.8 17.0 %all_to_all.16 = bf16[4,1,8,128,128]{4,3,2,1,0:T(8,128)(2,1)S(1)} all-to-all(bf16[4,1,8,128,128]{4,3,2,1,0:T(8,128)(2,1)S(1)} %copy.58), channel_id=1, replica_groups=mesh['section'=4,'sector'=4,'comp'=2] {'sector'}, dimensions={0} | all-to-all | bytes 2097152 | tf_op jit(solution)/shard_map/all_to_all | solution.py:48
  129.0 26.6 %all-gather.10.cloned.1.call-done = bf16[8,512,128]{2,0,1:T(8,128)(2,1)} async-done(((bf16[8,128,128]{2,0,1:T(8,128)(2,1)}), bf16[8,512,128]{2,0,1:T(8,128)(2,1)}) %all-gather.10.cloned.1.call-update) | async-done | bytes 1048592 | tf_op jit(solution)/shard_map/all_gather | solution.py:29
  155.6 6.2 %convert_bitcast_fusion = bf16[8,4,512,128]{3,0,1,2:T(8,128)(2,1)} fusion(bf16[8,512,128]{2,0,1:T(8,128)(2,1)} %all-gather.10.cloned.1.call-done, f32[3,4,8,8]{3,2,1,0:T(8,128)S(1)} %copy-done.1), kind=kOutput, calls=%fused_computation.9 | convolution fusion | flops 203423744 | bytes 5259264 | tf_op jit(solution)/shard_map/sdc,bcik->bdsik/dot_general | solution.py:26
  161.8 4.4 %fusion.19 = bf16[8,4,128,128]{3,2,0,1:T(8,128)(2,1)S(1)} fusion(bf16[8,4,512,128]{3,0,1,2:T(8,128)(2,1)} %convert_bitcast_fusion, bf16[512,4,128,1]{2,1,0,3:T(4,128)(2,1)S(1)} %get-tuple-element.8, bf16[1,1,128,4,128]{4,3,2,1,0:T(4,128)(2,1)S(1)} %get-tuple-element.11), kind=kOutput, calls=%fused_computation.25 | convolution fusion | flops 672137216 | bytes 5898240 | tf_op jit(solution)/shard_map/bdsok,ksl->bdsol/dot_general | solution.py:36
  166.2 0.9 fusion.20
  167.4 17.0 %all_to_all.17 = bf16[4,1,8,128,128]{4,3,2,1,0:T(8,128)(2,1)S(1)} all-to-all(bf16[4,1,8,128,128]{4,3,2,1,0:T(8,128)(2,1)S(1)} %copy.66), channel_id=1, replica_groups=mesh['section'=4,'sector'=4,'comp'=2] {'sector'}, dimensions={0} | all-to-all | bytes 2097152 | tf_op jit(solution)/shard_map/all_to_all | solution.py:48
  184.4 0.9 reduce_sum.48
  185.3 1.9 maximum_bitcast_fusion
  187.3 8.5 %reduce-scatter.2.cloned.1.call-done = bf16[4,128,128]{2,1,0:T(8,128)(2,1)} async-done(((bf16[8,128,128]{2,1,0:T(8,128)(2,1)}), bf16[4,128,128]{2,1,0:T(8,128)(2,1)}) %reduce-scatter.2.cloned.1.call-update) | async-done | bytes 131088 | tf_op jit(solution)/shard_map/reduce_scatter | solution.py:54
  (30 shorter events, 8.0 us)
Async XLA Ops:
  7.2 11.5 %copy-start = (bf16[3,1,512,4,128]{4,3,2,1,0:T(4,128)(2,1)S(1)}, bf16[3,1,512,4,128]{4,3,2,1,0:T(4,128)(2,1)}, u32[]{:S(2)}) copy-start(bf16[3,1,512,4,128]{4,3,2,1,0:T(4,128)(2,1)} %param.7) | copy-start | bytes 4718596
  7.2 34.8 %all-gather.6.cloned.1.call-start = ((), (), s32[]{:S(2)}) async-start(), calls=%async_computation.4 | async-start | bytes 1310720 | tf_op jit(solution)/shard_map/all_gather | solution.py:29
  11.2 87.8 %all-gather.8.cloned.1.call-start = ((), (), s32[]{:S(2)}) async-start(), calls=%async_computation.6 | async-start | bytes 1310720 | tf_op jit(solution)/shard_map/all_gather | solution.py:29
  53.0 46.0 %copy-start.1 = (f32[3,4,8,8]{3,2,1,0:T(8,128)S(1)}, f32[3,4,8,8]{3,2,1,0:T(8,128)}, u32[]{:S(2)}) copy-start(f32[3,4,8,8]{3,2,1,0:T(8,128)} %param.9) | copy-start | bytes 9220
  72.3 83.3 %all-gather.10.cloned.1.call-start = ((), (), s32[]{:S(2)}) async-start(), calls=%async_computation.7 | async-start | bytes 1310720 | tf_op jit(solution)/shard_map/all_gather | solution.py:29
  128.9 66.8 %reduce-scatter.2.cloned.1.call-start = ((), (), s32[]{:S(2)}) async-start(), calls=%async_computation.5 | async-start | bytes 393216 | tf_op jit(solution)/shard_map/reduce_scatter | solution.py:54
Sparse Core Ops, SparseCore 0:
  11.3 30.6 all-gather.5
  72.4 26.5 all-gather.7
  129.0 26.5 all-gather.9
  185.5 10.2 reduce-scatter.1
where the time goes:
time: 203 us; the launch traced here: 202 us
  waiting for transfers between devices  82.1 us (40%)
  blocking collectives  51 us (25%)
  matrix products  35 us (17%)
  between operations  13.9 us (7%)
  other arithmetic  11.3 us (6%)
  local copies, waits for them, and re-layouts  8.57 us (4%)
    all_gather x3, waiting for transfers between devices, local(): lax.all_gather(current, 'section', axis=2, tiled=True).astype(jnp.float32)  73.6 us
    all_to_all x3, blocking collectives, local(): lax.all_to_all(outgoing, 'sector', split_axis=0, concat_axis=0, tiled=True)  51 us
    dot_general x3, matrix products, local(): jnp.einsum('sdc,bcik->bdsik', weights, lax.all_gather(current, 'section',...  19.1 us
    dot_general x3, matrix products, local(): jnp.einsum('bdsok,ksl->bdsol', left_part, bra_tensor[site_index, 0], pref...  13.2 us
    reduce_scatter x1, waiting for transfers between devices, local(): lax.psum_scatter(batch_term.astype(jnp.bfloat16), 'comp', scatter_dimensi...  8.49 us
  transfers between devices with their start and end apart: 4, of which 4 were waited for; matrix products, arithmetic and copies ran while one was open for 6% of the time, Pallas kernels for 0%

commit v1 on v0

v1 whole, which is shorter than its diff:
```python
import functools

import jax
import jax.numpy as jnp
from jax import lax
from jax.experimental import pallas as pl
from jax.experimental.pallas import tpu as pltpu
from jax.sharding import PartitionSpec as P

GROUP = 2
REACH = 3


def sector_steps(sectors):
    if sectors <= 2 * REACH + 1:
        return list(range(sectors))
    return list(range(REACH + 1)) + [sectors - r for r in range(REACH, 0, -1)]


def kernel(
    sections, sectors, batches,
    env_ref, site_ref, bra_ref, mixing_ref, sizes_ref, targets_ref,
    out_ref, total_ref,
    gathered, outgoing, received, weights, acc, last, parts,
    ag_send, ag_recv, rt_send, rt_recv, tot_send, tot_recv, out_sem,
):
    sites, states, rows, full = site_ref.shape
    comps = env_ref.shape[0]
    width = env_ref.shape[2]
    steps = sector_steps(sectors)
    chunks = comps // GROUP
    share = comps // batches
    me_z = lax.axis_index("section")
    me_a = lax.axis_index("sector")
    me_b = lax.axis_index("comp")
    wrap = lambda value, count: lax.rem(value + count, count)
    forward = sections == 4

    barrier = pltpu.get_barrier_semaphore()
    greeted = 0
    for r in range(1, sections):
        pl.semaphore_signal(barrier, inc=1, device_id={"section": wrap(me_z + r, sections)},
                            device_id_type=pl.DeviceIdType.MESH)
        greeted += 1
    for r in steps[1:]:
        pl.semaphore_signal(barrier, inc=1, device_id={"sector": wrap(me_a + r, sectors)},
                            device_id_type=pl.DeviceIdType.MESH)
        greeted += 1
    for r in range(1, batches):
        pl.semaphore_signal(barrier, inc=1, device_id={"comp": wrap(me_b + r, batches)},
                            device_id_type=pl.DeviceIdType.MESH)
        greeted += 1
    pl.semaphore_wait(barrier, greeted)

    def gather_copy(t, q, owner, target, send_slot):
        block = gathered.at[t, owner, pl.ds(q * GROUP, GROUP)]
        return pltpu.make_async_remote_copy(
            src_ref=block, dst_ref=block,
            send_sem=ag_send.at[t, q, send_slot], recv_sem=ag_recv.at[t, q, owner],
            device_id={"section": target}, device_id_type=pl.DeviceIdType.MESH)

    def direct(z):
        near = jnp.abs(me_z - z) < sections - 1 if forward else True
        return jnp.logical_and(me_z != z, near)

    def gather_start(t, q):
        for z in range(sections):
            @pl.when(direct(z))
            def _():
                gather_copy(t, q, me_z, z, z).start()

    def gather_finish(t, q):
        if forward:
            for via, origin, end in ((1, 3, 0), (2, 0, 3)):
                @pl.when(me_z == via)
                def _():
                    gather_copy(t, q, origin, end, sections).wait_recv()
                    gather_copy(t, q, origin, end, sections).start()
        for z in range(sections):
            here = me_z != z
            if forward and z in (0, 3):
                here = jnp.logical_and(here, me_z != (2 if z == 0 else 1))

            @pl.when(here)
            def _():
                gather_copy(t, q, z, z, z).wait_recv()

    def gather_drain(t, q):
        for z in range(sections):
            @pl.when(direct(z))
            def _():
                gather_copy(t, q, me_z, z, z).wait_send()
        if forward:
            for via, origin, end in ((1, 3, 0), (2, 0, 3)):
                @pl.when(me_z == via)
                def _():
                    gather_copy(t, q, origin, end, sections).wait_send()

    def route_copy(t, q, j):
        chunk = pl.ds(q * GROUP, GROUP)
        return pltpu.make_async_remote_copy(
            src_ref=outgoing.at[t, j - 1, chunk], dst_ref=received.at[t, j, chunk],
            send_sem=rt_send.at[t, q, j], recv_sem=rt_recv.at[t, q, j],
            device_id={"sector": wrap(me_a + steps[j], sectors)},
            device_id_type=pl.DeviceIdType.MESH)

    def state_towards(t, source, target):
        state = jnp.int32(0)
        found = jnp.int32(0)
        for s in range(states):
            hit = targets_ref[t, source, s] == target
            state = jnp.where(hit, s, state)
            found = jnp.where(hit, 1, found)
        return state, found

    gathered[0, me_z] = env_ref[...]
    for q in range(chunks):
        gather_start(0, q)

    for t in range(sites):
        for j, step in enumerate(steps):
            target = wrap(me_a + step, sectors)
            state, found = state_towards(t, me_a, target)
            size_in = sizes_ref[t, me_a]
            size_out = sizes_ref[t + 1, target] * found
            o_ids = me_z * rows + lax.broadcasted_iota(jnp.int32, (rows, full), 0)
            i_ids = lax.broadcasted_iota(jnp.int32, (rows, full), 1)
            keep = jnp.logical_and(i_ids < size_in, o_ids < size_out)
            block = site_ref[t, state].astype(jnp.float32)
            weights[t, pl.ds(j * rows, rows)] = jnp.where(keep, block, 0.0).astype(jnp.bfloat16)

    def produce(t, q):
        columns = []
        for g in range(GROUP):
            column = gathered[t, :, q * GROUP + g].reshape(full, width)
            if t == 0:
                ids = lax.broadcasted_iota(jnp.int32, (full, width), 0)
                column = jnp.where(ids < sizes_ref[0, me_a], column.astype(jnp.float32), 0.0)
                column = column.astype(jnp.bfloat16)
            columns.append(column)
        left = jnp.dot(weights[t], jnp.concatenate(columns, axis=1),
                       preferred_element_type=jnp.float32).astype(jnp.bfloat16)
        for j in list(range(1, len(steps))) + [0]:
            state, _ = state_towards(t, me_a, wrap(me_a + steps[j], sectors))
            stacked = jnp.concatenate(
                [left[j * rows:(j + 1) * rows, g * width:(g + 1) * width] for g in range(GROUP)],
                axis=0)
            value = jnp.dot(stacked, bra_ref[t, state], preferred_element_type=jnp.float32)
            value = value.astype(jnp.bfloat16).reshape(GROUP, rows, width)
            if j:
                outgoing[t, j - 1, pl.ds(q * GROUP, GROUP)] = value
                route_copy(t, q, j).start()
            else:
                received[t, 0, pl.ds(q * GROUP, GROUP)] = value

    def route_finish(t, q):
        for j in range(1, len(steps)):
            route_copy(t, q, j).wait_recv()

    def combine(t, q, first, count, store):
        states_in = [state_towards(t, wrap(me_a - r, sectors), me_a)[0] for r in steps]
        factors = [[[mixing_ref[t, states_in[j], first + i, q * GROUP + g]
                     for g in range(GROUP)] for j in range(len(steps))] for i in range(count)]

        def tile(r, carry):
            where = pl.ds(pl.multiple_of(r * 32, 32), 32)
            terms = [[received[t, j, q * GROUP + g, where].astype(jnp.float32)
                      for g in range(GROUP)] for j in range(len(steps))]
            for i in range(count):
                value = None if q == 0 else acc[first + i, where]
                for j in range(len(steps)):
                    for g in range(GROUP):
                        term = terms[j][g] * factors[i][j][g]
                        value = term if value is None else value + term
                store(first + i, where, value)
            return carry

        lax.fori_loop(0, rows // 32, tile, 0)

    def keep_sum(d, where, value):
        acc[d, where] = value

    def total_copy(r):
        peer = wrap(me_b + r, batches)
        return pltpu.make_async_remote_copy(
            src_ref=last.at[pl.ds(peer * share, share)], dst_ref=parts.at[r - 1],
            send_sem=tot_send.at[r - 1], recv_sem=tot_recv.at[r - 1],
            device_id={"comp": peer}, device_id_type=pl.DeviceIdType.MESH)

    out_copies = []
    for t in range(sites):
        for q in range(chunks):
            gather_finish(t, q)
            produce(t, q)
            if q:
                route_finish(t, q - 1)
                for first in range(0, comps, 4):
                    combine(t, q - 1, first, 4, keep_sum)
        q = chunks - 1
        route_finish(t, q)
        if t + 1 < sites:
            def keep_next(d, where, value, t=t):
                gathered[t + 1, me_z, d, where] = value.astype(jnp.bfloat16)

            for nxt in range(chunks):
                combine(t, q, nxt * GROUP, GROUP, keep_next)
                gather_start(t + 1, nxt)
            copy = pltpu.make_async_copy(gathered.at[t + 1, me_z], out_ref.at[t, 0, :, 0], out_sem.at[t])
        else:
            def keep_last(d, where, value):
                last[d, where] = value.astype(jnp.bfloat16)

            for r in list(range(1, batches)) + [0]:
                combine(t, q, wrap(me_b + r, batches) * share, share, keep_last)
                if r:
                    total_copy(r).start()
            copy = pltpu.make_async_copy(last, out_ref.at[t, 0, :, 0], out_sem.at[t])
        copy.start()
        out_copies.append(copy)

    for t in range(sites):
        for q in range(chunks):
            gather_drain(t, q)
            for j in range(1, len(steps)):
                route_copy(t, q, j).wait_send()
    summed = last[pl.ds(me_b * share, share)].astype(jnp.float32)
    for r in range(1, batches):
        total_copy(r).wait_recv()
        summed = summed + parts[r - 1].astype(jnp.float32)
    total_ref[:, 0] = summed.astype(jnp.bfloat16)
    for r in range(1, batches):
        total_copy(r).wait_send()
    for copy in out_copies:
        copy.wait()


def local(sections, sectors, batches, env_in, site_tensor, bra_tensor, mixing, sector_sizes, targets):
    env = env_in[0, :, 0]
    site = jnp.transpose(site_tensor[:, 0], (0, 2, 3, 1))
    bra = jnp.transpose(bra_tensor[:, 0], (0, 2, 1, 3))
    sites, states, rows, full = site.shape
    comps, _, width = env.shape
    slots = len(sector_steps(sectors))
    chunks = comps // GROUP
    share = comps // batches
    vmem = pl.BlockSpec(memory_space=pltpu.VMEM)
    smem = pl.BlockSpec(memory_space=pltpu.SMEM)
    dma = pltpu.SemaphoreType.DMA
    return pl.pallas_call(
        functools.partial(kernel, sections, sectors, batches),
        out_shape=(
            jax.ShapeDtypeStruct((sites, 1, comps, 1, rows, width), jnp.bfloat16),
            jax.ShapeDtypeStruct((share, 1, rows, width), jnp.bfloat16),
        ),
        in_specs=[vmem, vmem, vmem, smem, smem, smem],
        out_specs=(pl.BlockSpec(memory_space=pl.ANY), vmem),
        scratch_shapes=[
            pltpu.VMEM((sites, sections, comps, rows, width), jnp.bfloat16),
            pltpu.VMEM((sites, max(slots - 1, 1), comps, rows, width), jnp.bfloat16),
            pltpu.VMEM((sites, slots, comps, rows, width), jnp.bfloat16),
            pltpu.VMEM((sites, slots * rows, full), jnp.bfloat16),
            pltpu.VMEM((comps, rows, width), jnp.float32),
            pltpu.VMEM((comps, rows, width), jnp.bfloat16),
            pltpu.VMEM((max(batches - 1, 1), share, rows, width), jnp.bfloat16),
            dma((sites, chunks, sections + 1)),
            dma((sites, chunks, sections)),
            dma((sites, chunks, slots)),
            dma((sites, chunks, slots)),
            dma((max(batches - 1, 1),)),
            dma((max(batches - 1, 1),)),
            dma((sites,)),
        ],
        compiler_params=pltpu.CompilerParams(
            collective_id=0, has_side_effects=True, vmem_limit_bytes=40 * 1024 * 1024),
    )(env, site, bra, mixing, sector_sizes, targets)


def solution(mesh):
    in_specs = (
        P("comp", None, "sector", "section", None),
        P(None, "sector", None, None, "section"),
        P(None, "sector", None, None, None),
        P(),
        P(),
        P(),
    )
    out_specs = (
        P(None, "comp", None, "sector", "section", None),
        P("comp", "sector", "section", None),
    )
    body = functools.partial(local, mesh.shape["section"], mesh.shape["sector"], mesh.shape["comp"])
    return jax.shard_map(body, mesh=mesh, in_specs=in_specs, out_specs=out_specs, check_vma=False)
```

time: 203 us -> 92.4 us (0.46)
  Pallas kernels: 0 us -> 86.1 us
  waiting for transfers between devices: 82.1 us -> 0 us
  blocking collectives: 51 us -> 0 us
  matrix products: 35 us -> 0 us
  between operations: 13.9 us -> 0.72 us
  other arithmetic: 11.3 us -> 0 us
  local copies, waits for them, and re-layouts: 8.57 us -> 5.3 us
    pallas_call x0 -> x1, Pallas kernels: none -> 86.1 us  [local(): pl.pallas_call(functools.partial(kernel, sections, sectors, batches), out...]
    all_gather x3 -> x0, waiting for transfers between devices: 73.6 us -> none  [local(): lax.all_gather(current, 'section', axis=2, tiled=True).astype(jnp.float32)]
    all_to_all x3 -> x0, blocking collectives: 51 us -> none  [local(): lax.all_to_all(outgoing, 'sector', split_axis=0, concat_axis=0, tiled=True)]
    dot_general x9 -> x0, matrix products: 35 us -> none  [the longest x3 19.1 us: local(): jnp.einsum('sdc,bcik->bdsik', weights, lax.all_gather(current, 'section',...]
    reduce_scatter x1 -> x0, waiting for transfers between devices: 8.49 us -> none  [local(): lax.psum_scatter(batch_term.astype(jnp.bfloat16), 'comp', scatter_dimensi...]
    unnamed x4 -> x12, local copies, waits for them, and re-layouts: 0.01 us -> 5.3 us
    mul x2 -> x0, other arithmetic: 4.69 us -> none  [the longest x1 2.84 us: local(): site_tensor[site_index, 0] * keep_in[:, None, None] * keep_out[None, :, :]]
    convert_element_type x4 -> x0, other arithmetic: 2.62 us -> none  [the longest x2 1.91 us: local(): (row_ids < sector_sizes[site_index, sector_index]).astype(jnp.bfloat16)]
  transfers between devices with their start and end apart: 4 -> 0, of which waited for: 4 -> 0; matrix products, arithmetic and copies ran while one was open for 6% -> 0% of each run, Pallas kernels for 0% -> 0%
where the time goes in v1:
time: 92.4 us; the launch traced here: 92.1 us
  Pallas kernels  86.1 us (93%)
  local copies, waits for them, and re-layouts  5.3 us (6%)
    pallas_call x1, Pallas kernels, local(): pl.pallas_call(functools.partial(kernel, sections, sectors, batches), out...  86.1 us
    unnamed x12, local copies, waits for them, and re-layouts  5.3 us

profile of v1, /device:TPU:0, one launch (start us, length us, event | category | flops | bytes accessed | tf_op | source)
XLA Modules:
  0.0 92.1 jit_solution(7956122542655339407)
XLA Ops:
  0.6 1.1 %copy.11 = bf16[3,1,128,4,128]{4,2,3,0,1:T(8,128)(2,1)S(1)} copy(bf16[3,1,128,4,128]{4,3,2,1,0:T(4,128)(2,1)} %param.8) | data formatting | bytes 786432 | tf_op args[2]
  1.7 0.0 copy-start
  1.7 0.0 copy-start.1
  1.7 0.0 copy-start.2
  1.7 0.0 copy-start.3
  1.7 2.7 %copy.8 = bf16[3,1,512,4,128]{2,4,3,0,1:T(8,128)(2,1)S(1)} copy(bf16[3,1,512,4,128]{4,3,2,1,0:T(4,128)(2,1)} %param.7) | data formatting | bytes 3145728 | tf_op args[1]
  4.4 0.0 copy-done
  4.4 0.0 copy-done.1
  4.5 0.0 copy-done.2
  4.5 0.0 copy-done.3
  4.5 86.1 %shard_map.77 = (bf16[3,1,8,1,128,128]{5,4,3,2,1,0:T(8,128)(2,1)S(1)}, bf16[4,1,128,128]{3,2,1,0:T(8,128)(2,1)S(1)}) custom-call(bf16[8,128,128]{2,1,0:T(8,128)(2,1)S(1)} %bitcast.11, bf16[3,4,128,512]{3,2,1,0:T(8,128)(2,1)S(1)} %bitcast.9, bf16[3,4,128,128]{3,2,1,0:T(8,128)(2,1)S(1)} %bitcast.10, f32[3,4,8,8]{3,2,1,0:T(8,128)S(1)} %copy-done.1, ...), custom_call_target="tpu_custom_call" | custom-call | tf_op jit(solution)/shard_map/pallas_call | solution.py:249
  90.6 0.9 copy.14
  91.5 0.7 copy.15
Async XLA Ops:
  1.7 2.7 %copy-start = (bf16[1,8,1,128,128]{4,3,2,1,0:T(8,128)(2,1)S(1)}, bf16[1,8,1,128,128]{4,3,2,1,0:T(8,128)(2,1)}, u32[]{:S(2)}) copy-start(bf16[1,8,1,128,128]{4,3,2,1,0:T(8,128)(2,1)} %param.6) | copy-start | bytes 786436
  1.7 2.7 %copy-start.1 = (f32[3,4,8,8]{3,2,1,0:T(8,128)S(1)}, f32[3,4,8,8]{3,2,1,0:T(8,128)}, u32[]{:S(2)}) copy-start(f32[3,4,8,8]{3,2,1,0:T(8,128)} %mixing_ref.1) | copy-start | bytes 9220
  1.7 2.7 %copy-start.2 = (s32[3,4,4]{2,1,0:T(4,128)S(1)}, s32[3,4,4]{2,1,0:T(4,128)}, u32[]{:S(2)}) copy-start(s32[3,4,4]{2,1,0:T(4,128)} %targets_ref.1) | copy-start | bytes 580
  1.7 2.7 %copy-start.3 = (s32[4,4]{1,0:T(4,128)S(1)}, s32[4,4]{1,0:T(4,128)}, u32[]{:S(2)}) copy-start(s32[4,4]{1,0:T(4,128)} %sizes_ref.1) | copy-start | bytes 196

commit v2 on v1

--- a/solution.py
+++ b/solution.py
@@ -7,7 +7,9 @@
 from jax.experimental.pallas import tpu as pltpu
 from jax.sharding import PartitionSpec as P
 
-GROUP = 2
+LEAD = 1
+SIZES = (2, 2, 2, 2)
+WINDOW = 9
 REACH = 3
 
 
@@ -28,7 +30,8 @@
     comps = env_ref.shape[0]
     width = env_ref.shape[2]
     steps = sector_steps(sectors)
-    chunks = comps // GROUP
+    chunks = len(SIZES)
+    starts = [sum(SIZES[:q]) for q in range(chunks)]
     share = comps // batches
     me_z = lax.axis_index("section")
     me_a = lax.axis_index("sector")
@@ -53,7 +56,7 @@
     pl.semaphore_wait(barrier, greeted)
 
     def gather_copy(t, q, owner, target, send_slot):
-        block = gathered.at[t, owner, pl.ds(q * GROUP, GROUP)]
+        block = gathered.at[t, owner, pl.ds(starts[q], SIZES[q])]
         return pltpu.make_async_remote_copy(
             src_ref=block, dst_ref=block,
             send_sem=ag_send.at[t, q, send_slot], recv_sem=ag_recv.at[t, q, owner],
@@ -63,19 +66,33 @@
         near = jnp.abs(me_z - z) < sections - 1 if forward else True
         return jnp.logical_and(me_z != z, near)
 
-    def gather_start(t, q):
+    inner = jnp.logical_or(me_z == 1, me_z == 2)
+
+    def gather_start(t, q, late=False):
         for z in range(sections):
-            @pl.when(direct(z))
+            chosen = direct(z)
+            if forward and late:
+                chosen = jnp.logical_and(chosen, inner)
+            elif forward and q >= WINDOW:
+                chosen = jnp.logical_and(chosen, jnp.logical_not(inner))
+
+            @pl.when(chosen)
             def _():
                 gather_copy(t, q, me_z, z, z).start()
 
+    def gather_forward(t, q):
+        for via, origin, end in ((1, 3, 0), (2, 0, 3)):
+            @pl.when(me_z == via)
+            def _():
+                gather_copy(t, q, origin, end, sections).wait_recv()
+                gather_copy(t, q, origin, end, sections).start()
+        if q + WINDOW < chunks:
+            gather_start(t, q + WINDOW, late=True)
+
     def gather_finish(t, q):
         if forward:
-            for via, origin, end in ((1, 3, 0), (2, 0, 3)):
-                @pl.when(me_z == via)
-                def _():
-                    gather_copy(t, q, origin, end, sections).wait_recv()
-                    gather_copy(t, q, origin, end, sections).start()
+            for ahead in range(q + LEAD if q else 0, min(q + LEAD + 1, chunks)):
+                gather_forward(t, ahead)
         for z in range(sections):
             here = me_z != z
             if forward and z in (0, 3):
@@ -97,7 +114,7 @@
                     gather_copy(t, q, origin, end, sections).wait_send()
 
     def route_copy(t, q, j):
-        chunk = pl.ds(q * GROUP, GROUP)
+        chunk = pl.ds(starts[q], SIZES[q])
         return pltpu.make_async_remote_copy(
             src_ref=outgoing.at[t, j - 1, chunk], dst_ref=received.at[t, j, chunk],
             send_sem=rt_send.at[t, q, j], recv_sem=rt_recv.at[t, q, j],
@@ -131,8 +148,8 @@
 
     def produce(t, q):
         columns = []
-        for g in range(GROUP):
-            column = gathered[t, :, q * GROUP + g].reshape(full, width)
+        for g in range(SIZES[q]):
+            column = gathered[t, :, starts[q] + g].reshape(full, width)
             if t == 0:
                 ids = lax.broadcasted_iota(jnp.int32, (full, width), 0)
                 column = jnp.where(ids < sizes_ref[0, me_a], column.astype(jnp.float32), 0.0)
@@ -143,15 +160,15 @@
         for j in list(range(1, len(steps))) + [0]:
             state, _ = state_towards(t, me_a, wrap(me_a + steps[j], sectors))
             stacked = jnp.concatenate(
-                [left[j * rows:(j + 1) * rows, g * width:(g + 1) * width] for g in range(GROUP)],
+                [left[j * rows:(j + 1) * rows, g * width:(g + 1) * width] for g in range(SIZES[q])],
                 axis=0)
             value = jnp.dot(stacked, bra_ref[t, state], preferred_element_type=jnp.float32)
-            value = value.astype(jnp.bfloat16).reshape(GROUP, rows, width)
+            value = value.astype(jnp.bfloat16).reshape(SIZES[q], rows, width)
             if j:
-                outgoing[t, j - 1, pl.ds(q * GROUP, GROUP)] = value
+                outgoing[t, j - 1, pl.ds(starts[q], SIZES[q])] = value
                 route_copy(t, q, j).start()
             else:
-                received[t, 0, pl.ds(q * GROUP, GROUP)] = value
+                received[t, 0, pl.ds(starts[q], SIZES[q])] = value
 
     def route_finish(t, q):
         for j in range(1, len(steps)):
@@ -159,17 +176,17 @@
 
     def combine(t, q, first, count, store):
         states_in = [state_towards(t, wrap(me_a - r, sectors), me_a)[0] for r in steps]
-        factors = [[[mixing_ref[t, states_in[j], first + i, q * GROUP + g]
-                     for g in range(GROUP)] for j in range(len(steps))] for i in range(count)]
+        factors = [[[mixing_ref[t, states_in[j], first + i, starts[q] + g]
+                     for g in range(SIZES[q])] for j in range(len(steps))] for i in range(count)]
 
         def tile(r, carry):
             where = pl.ds(pl.multiple_of(r * 32, 32), 32)
-            terms = [[received[t, j, q * GROUP + g, where].astype(jnp.float32)
-                      for g in range(GROUP)] for j in range(len(steps))]
+            terms = [[received[t, j, starts[q] + g, where].astype(jnp.float32)
+                      for g in range(SIZES[q])] for j in range(len(steps))]
             for i in range(count):
                 value = None if q == 0 else acc[first + i, where]
                 for j in range(len(steps)):
-                    for g in range(GROUP):
+                    for g in range(SIZES[q]):
                         term = terms[j][g] * factors[i][j][g]
                         value = term if value is None else value + term
                 store(first + i, where, value)
@@ -203,7 +220,7 @@
                 gathered[t + 1, me_z, d, where] = value.astype(jnp.bfloat16)
 
             for nxt in range(chunks):
-                combine(t, q, nxt * GROUP, GROUP, keep_next)
+                combine(t, q, starts[nxt], SIZES[nxt], keep_next)
                 gather_start(t + 1, nxt)
             copy = pltpu.make_async_copy(gathered.at[t + 1, me_z], out_ref.at[t, 0, :, 0], out_sem.at[t])
         else:
@@ -241,7 +258,7 @@
     sites, states, rows, full = site.shape
     comps, _, width = env.shape
     slots = len(sector_steps(sectors))
-    chunks = comps // GROUP
+    chunks = len(SIZES)
     share = comps // batches
     vmem = pl.BlockSpec(memory_space=pltpu.VMEM)
     smem = pl.BlockSpec(memory_space=pltpu.SMEM)

time: 92.4 us -> 91.6 us (level)
  no operation moved by 1% of the time
where the time goes in v2:
time: 91.6 us; the launch traced here: 91.4 us
  Pallas kernels  85.4 us (93%)
  local copies, waits for them, and re-layouts  5.3 us (6%)
    pallas_call x1, Pallas kernels, local(): pl.pallas_call(functools.partial(kernel, sections, sectors, batches), out...  85.4 us
    unnamed x12, local copies, waits for them, and re-layouts  5.3 us

profile of v2, /device:TPU:0, one launch (start us, length us, event | category | flops | bytes accessed | tf_op | source)
XLA Modules:
  0.0 91.4 jit_solution(12251725532992656488)
XLA Ops:
  0.6 1.1 %copy.11 = bf16[3,1,128,4,128]{4,2,3,0,1:T(8,128)(2,1)S(1)} copy(bf16[3,1,128,4,128]{4,3,2,1,0:T(4,128)(2,1)} %param.8) | data formatting | bytes 786432 | tf_op args[2]
  1.7 0.0 copy-start
  1.7 0.0 copy-start.1
  1.7 0.0 copy-start.2
  1.7 0.0 copy-start.3
  1.7 2.7 %copy.8 = bf16[3,1,512,4,128]{2,4,3,0,1:T(8,128)(2,1)S(1)} copy(bf16[3,1,512,4,128]{4,3,2,1,0:T(4,128)(2,1)} %param.7) | data formatting | bytes 3145728 | tf_op args[1]
  4.4 0.0 copy-done
  4.4 0.0 copy-done.1
  4.5 0.0 copy-done.2
  4.5 0.0 copy-done.3
  4.5 85.4 %shard_map.77 = (bf16[3,1,8,1,128,128]{5,4,3,2,1,0:T(8,128)(2,1)S(1)}, bf16[4,1,128,128]{3,2,1,0:T(8,128)(2,1)S(1)}) custom-call(bf16[8,128,128]{2,1,0:T(8,128)(2,1)S(1)} %bitcast.11, bf16[3,4,128,512]{3,2,1,0:T(8,128)(2,1)S(1)} %bitcast.9, bf16[3,4,128,128]{3,2,1,0:T(8,128)(2,1)S(1)} %bitcast.10, f32[3,4,8,8]{3,2,1,0:T(8,128)S(1)} %copy-done.1, ...), custom_call_target="tpu_custom_call" | custom-call | tf_op jit(solution)/shard_map/pallas_call | solution.py:266
  89.9 0.9 copy.14
  90.8 0.7 copy.15
Async XLA Ops:
  1.7 2.7 %copy-start = (bf16[1,8,1,128,128]{4,3,2,1,0:T(8,128)(2,1)S(1)}, bf16[1,8,1,128,128]{4,3,2,1,0:T(8,128)(2,1)}, u32[]{:S(2)}) copy-start(bf16[1,8,1,128,128]{4,3,2,1,0:T(8,128)(2,1)} %param.6) | copy-start | bytes 786436
  1.7 2.7 %copy-start.1 = (f32[3,4,8,8]{3,2,1,0:T(8,128)S(1)}, f32[3,4,8,8]{3,2,1,0:T(8,128)}, u32[]{:S(2)}) copy-start(f32[3,4,8,8]{3,2,1,0:T(8,128)} %mixing_ref.1) | copy-start | bytes 9220
  1.7 2.7 %copy-start.2 = (s32[3,4,4]{2,1,0:T(4,128)S(1)}, s32[3,4,4]{2,1,0:T(4,128)}, u32[]{:S(2)}) copy-start(s32[3,4,4]{2,1,0:T(4,128)} %targets_ref.1) | copy-start | bytes 580
  1.7 2.7 %copy-start.3 = (s32[4,4]{1,0:T(4,128)S(1)}, s32[4,4]{1,0:T(4,128)}, u32[]{:S(2)}) copy-start(s32[4,4]{1,0:T(4,128)} %sizes_ref.1) | copy-start | bytes 196
